TPU v7x, 32 devices: a whole 2x2x4 slice. The times are simulated.
32 devices in a mesh: blk: 8 (over z, y), col: 4 (over x, core).
Axes of the slice: x: 2, y: 2, z: 4, core: 2. Of those that a mesh axis runs over, the one named last changes fastest.
Arguments:
- start_panel: float32 [128, 16384], P('col', 'blk'), may hold values from -6 to 6
- tile_values: float32 [192, 128, 128], P('blk'), may hold values from -0.3125 to 0.3125
- tile_rows: int32 [192], P('blk'), may hold values from 0 to 127, as said below
- tile_cols: int32 [192], P('blk'), may hold values from 0 to 127, as said below
- tile_counts: int32 [8], P('blk'), may hold values from 5 to 24, as said below
Outputs:
- ortho_panel: float32 [128, 16384], P('col', 'blk')
- gram_factor: float32 [128, 128], replicated
Inputs may be any that keep to these rules, and one draw needn't show every extreme that they name: `tile_rows`: slot s has a row block among those of blk index s // 24, that is s // 24 * 16 up to s // 24 * 16 + 15. `tile_cols`: slot s has a column block among those of blk indices s // 24 + o for o from -2 to 2, taken modulo the number of blk indices; slot j of each blk index with j < 5 takes o = j - 2. `tile_counts`: some blk index has all 24 slots live; every blk index has 5 or more.
All inputs are finite; a program needn't handle non-finite values.
Results may differ from a plain program's by a relative error of at most 0.0003.
Values sent between devices are 32-bit elements; how exact they have to be, the bound alone decides.
A program may use at most 64 MiB of HBM per device.

v0:
```python
import jax
import jax.numpy as jnp
from jax import lax
from jax.sharding import PartitionSpec as P

BS = 128
K = 128
RB_DEV = 16
TILE_CAP = 24
REACH = 2
DEGREE = 4


def shifted(value, axis, steps):
    count = lax.axis_size(axis)
    pairs = [(source, (source + steps) % count) for source in range(count)]
    return lax.ppermute(value, axis, pairs)


def band_window(panel):
    lower = []
    current = panel
    for offset in range(REACH):
        current = shifted(current, "blk", 1)
        lower.append(current)
    higher = []
    current = panel
    for offset in range(REACH):
        current = shifted(current, "blk", -1)
        higher.append(current)
    pieces = lower[::-1] + [panel] + higher
    return jnp.concatenate(pieces, axis=1)


def apply_graph(panel, tile_values, local_cols, row_table, live):
    window = band_window(panel)
    width = panel.shape[0]
    blocks = window.reshape(width, (2 * REACH + 1) * RB_DEV, BS)
    piece = blocks[:, local_cols, :]
    contrib = jnp.einsum("ktb,tab->kta", piece, tile_values, precision=lax.Precision.HIGHEST)
    contrib = jnp.where(live[None, :, None], contrib, jnp.zeros_like(contrib))
    summed = jnp.einsum("kta,tr->kra", contrib, row_table, precision=lax.Precision.HIGHEST)
    return summed.reshape(width, RB_DEV * BS)


def per_device(start_panel, tile_values, tile_rows, tile_cols, tile_counts):
    position = lax.axis_index("blk")
    cycle_count = lax.axis_size("blk")
    local_cols = (
        tile_cols // RB_DEV - position + REACH + cycle_count
    ) % cycle_count * RB_DEV + tile_cols % RB_DEV
    local_rows = tile_rows - position * RB_DEV
    row_table = (local_rows[:, None] == jnp.arange(RB_DEV, dtype=jnp.int32)[None, :]).astype(
        jnp.float32
    )
    live = jnp.arange(TILE_CAP, dtype=jnp.int32) < tile_counts[0]
    previous = start_panel
    current = apply_graph(start_panel, tile_values, local_cols, row_table, live)
    for step in range(DEGREE - 1):
        upcoming = 2.0 * apply_graph(current, tile_values, local_cols, row_table, live) - previous
        previous, current = (current, upcoming)
    all_columns = lax.all_gather(current, "col", axis=0, tiled=True)
    partial_rows = jnp.dot(current, all_columns.T, precision=lax.Precision.HIGHEST)
    own_rows = lax.psum(partial_rows, "blk")
    gram = lax.all_gather(own_rows, "col", axis=0, tiled=True)
    factor = jnp.linalg.cholesky(gram)
    total_rows = current.shape[1] * cycle_count
    scale = jnp.sqrt(jnp.asarray(total_rows, jnp.float32))
    inverse = lax.linalg.triangular_solve(
        factor, jnp.eye(K, dtype=jnp.float32), left_side=True, lower=True
    )
    width = current.shape[0]
    inverse_rows = lax.dynamic_slice_in_dim(inverse, lax.axis_index("col") * width, width, 0)
    ortho_panel = jnp.dot(inverse_rows, all_columns, precision=lax.Precision.HIGHEST) * scale
    return (ortho_panel, factor / scale)


def solution(mesh):
    in_specs = (P("col", "blk"), P("blk", None, None), P("blk"), P("blk"), P("blk"))
    out_specs = (P("col", "blk"), P())
    return jax.shard_map(
        per_device, mesh=mesh, in_specs=in_specs, out_specs=out_specs, check_vma=False
    )
```

profile of v0, /device:TPU:0, one launch (start us, length us, event | category | flops | bytes accessed | tf_op | source)
XLA Modules:
  0.0 229.9 jit_solution(8815334889623607098)
XLA Ops:
  7.2 3.0 %collective-permute-start = (f32[32,2048]{1,0:T(8,128)}, f32[32,2048]{1,0:T(8,128)S(1)}, u32[]{:S(2)}, u32[]{:S(2)}) collective-permute-start(f32[32,2048]{1,0:T(8,128)} %param.5), channel_id=1, source_target_pairs={{0,4},{4,8},{8,12},{12,16},{16,20},{20,24},{24,28},{28,0},{1,5},{5... | collective-permute-start | bytes 786440 | tf_op jit(solution)/shard_map/ppermute | solution.py:17
  10.2 3.1 %collective-permute-start.2 = (f32[32,2048]{1,0:T(8,128)}, f32[32,2048]{1,0:T(8,128)S(1)}, u32[]{:S(2)}, u32[]{:S(2)}) collective-permute-start(f32[32,2048]{1,0:T(8,128)} %param.5), channel_id=1, source_target_pairs={{0,28},{4,0},{8,4},{12,8},{16,12},{20,16},{24,20},{28,24},{1,29},{... | collective-permute-start | bytes 786440 | tf_op jit(solution)/shard_map/ppermute | solution.py:17
  14.7 7.0 %collective-permute-done = f32[32,2048]{1,0:T(8,128)S(1)} collective-permute-done((f32[32,2048]{1,0:T(8,128)}, f32[32,2048]{1,0:T(8,128)S(1)}, u32[]{:S(2)}, u32[]{:S(2)}) %collective-permute-start) | collective-permute-done | bytes 262176 | tf_op jit(solution)/shard_map/ppermute | solution.py:17
  24.8 3.0 %collective-permute-start.3 = (f32[32,2048]{1,0:T(8,128)S(1)}, f32[32,2048]{1,0:T(8,128)S(1)}, u32[]{:S(2)}, u32[]{:S(2)}) collective-permute-start(f32[32,2048]{1,0:T(8,128)S(1)} %collective-permute-done.2), channel_id=1, source_target_pairs={{0,28},{4,0},{8,4},{12,8},{16,12},{20,16},{24,20},{28,24},{1,29},{... | collective-permute-start | bytes 786440 | tf_op jit(solution)/shard_map/ppermute | solution.py:17
  27.8 6.6 %collective-permute-done.1 = f32[32,2048]{1,0:T(8,128)S(1)} collective-permute-done((f32[32,2048]{1,0:T(8,128)S(1)}, f32[32,2048]{1,0:T(8,128)S(1)}, u32[]{:S(2)}, u32[]{:S(2)}) %collective-permute-start.1) | collective-permute-done | bytes 262176 | tf_op jit(solution)/shard_map/ppermute | solution.py:17
  42.0 4.0 %collective-permute-start.6 = (f32[32,2048]{1,0:T(8,128)S(1)}, f32[32,2048]{1,0:T(8,128)S(1)}, u32[]{:S(2)}, u32[]{:S(2)}) collective-permute-start(f32[32,2048]{1,0:T(8,128)S(1)} %bitcast.100), channel_id=1, source_target_pairs={{0,28},{4,0},{8,4},{12,8},{16,12},{20,16},{24,20},{28,24},{1,29},{... | collective-permute-start | bytes 786440 | tf_op jit(solution)/shard_map/ppermute | solution.py:17
  46.0 5.9 %collective-permute-done.4 = f32[32,2048]{1,0:T(8,128)S(1)} collective-permute-done((f32[32,2048]{1,0:T(8,128)S(1)}, f32[32,2048]{1,0:T(8,128)S(1)}, u32[]{:S(2)}, u32[]{:S(2)}) %collective-permute-start.4) | collective-permute-done | bytes 262176 | tf_op jit(solution)/shard_map/ppermute | solution.py:17
  54.6 4.8 %collective-permute-start.7 = (f32[32,2048]{1,0:T(8,128)S(1)}, f32[32,2048]{1,0:T(8,128)S(1)}, u32[]{:S(2)}, u32[]{:S(2)}) collective-permute-start(f32[32,2048]{1,0:T(8,128)S(1)} %collective-permute-done.6), channel_id=1, source_target_pairs={{0,28},{4,0},{8,4},{12,8},{16,12},{20,16},{24,20},{28,24},{1,29},{... | collective-permute-start | bytes 786440 | tf_op jit(solution)/shard_map/ppermute | solution.py:17
  59.3 3.3 %collective-permute-done.5 = f32[32,2048]{1,0:T(8,128)S(1)} collective-permute-done((f32[32,2048]{1,0:T(8,128)S(1)}, f32[32,2048]{1,0:T(8,128)S(1)}, u32[]{:S(2)}, u32[]{:S(2)}) %collective-permute-start.5) | collective-permute-done | bytes 262176 | tf_op jit(solution)/shard_map/ppermute | solution.py:17
  62.8 3.1 %collective-permute-done.7 = f32[32,2048]{1,0:T(8,128)S(1)} collective-permute-done((f32[32,2048]{1,0:T(8,128)S(1)}, f32[32,2048]{1,0:T(8,128)S(1)}, u32[]{:S(2)}, u32[]{:S(2)}) %collective-permute-start.7) | collective-permute-done | bytes 262176 | tf_op jit(solution)/shard_map/ppermute | solution.py:17
  71.0 4.0 %collective-permute-start.10 = (f32[32,2048]{1,0:T(8,128)S(1)}, f32[32,2048]{1,0:T(8,128)S(1)}, u32[]{:S(2)}, u32[]{:S(2)}) collective-permute-start(f32[32,2048]{1,0:T(8,128)S(1)} %bitcast_subtract_fusion.2), channel_id=1, source_target_pairs={{0,28},{4,0},{8,4},{12,8},{16,12},{20,16},{24,20},{28,24},{1,29},{... | collective-permute-start | bytes 786440 | tf_op jit(solution)/shard_map/ppermute | solution.py:17
  75.0 7.8 %collective-permute-done.8 = f32[32,2048]{1,0:T(8,128)S(1)} collective-permute-done((f32[32,2048]{1,0:T(8,128)S(1)}, f32[32,2048]{1,0:T(8,128)S(1)}, u32[]{:S(2)}, u32[]{:S(2)}) %collective-permute-start.8) | collective-permute-done | bytes 262176 | tf_op jit(solution)/shard_map/ppermute | solution.py:17
  85.5 7.4 %collective-permute-start.11 = (f32[32,2048]{1,0:T(8,128)S(1)}, f32[32,2048]{1,0:T(8,128)S(1)}, u32[]{:S(2)}, u32[]{:S(2)}) collective-permute-start(f32[32,2048]{1,0:T(8,128)S(1)} %collective-permute-done.10), channel_id=1, source_target_pairs={{0,28},{4,0},{8,4},{12,8},{16,12},{20,16},{24,20},{28,24},{1,29},{... | collective-permute-start | bytes 786440 | tf_op jit(solution)/shard_map/ppermute | solution.py:17
  93.1 5.4 %collective-permute-done.11 = f32[32,2048]{1,0:T(8,128)S(1)} collective-permute-done((f32[32,2048]{1,0:T(8,128)S(1)}, f32[32,2048]{1,0:T(8,128)S(1)}, u32[]{:S(2)}, u32[]{:S(2)}) %collective-permute-start.11) | collective-permute-done | bytes 262176 | tf_op jit(solution)/shard_map/ppermute | solution.py:17
  100.0 3.5 %fusion.1 = f32[32,24,128]{2,0,1:T(8,128)S(1)} fusion(f32[24,128,128]{2,1,0:T(8,128)S(1)} %copy-done, f32[24,32,128]{2,1,0:T(8,128)} %gather_fusion.2, pred[24]{0:T(512)(128)(4,1)S(1)} %iota_compare_fusion.4), kind=kOutput, calls=%fused_computation.11 | convolution fusion | flops 151093248 | bytes 2359320 | tf_op jit(solution)/shard_map/ktb,tab->kta/dot_general | solution.py:40
  104.3 4.7 %collective-permute-start.14 = (f32[32,2048]{1,0:T(8,128)S(1)}, f32[32,2048]{1,0:T(8,128)S(1)}, u32[]{:S(2)}, u32[]{:S(2)}) collective-permute-start(f32[32,2048]{1,0:T(8,128)S(1)} %bitcast_subtract_fusion.1), channel_id=1, source_target_pairs={{0,28},{4,0},{8,4},{12,8},{16,12},{20,16},{24,20},{28,24},{1,29},{... | collective-permute-start | bytes 786440 | tf_op jit(solution)/shard_map/ppermute | solution.py:17
  109.0 6.9 %collective-permute-done.12 = f32[32,2048]{1,0:T(8,128)S(1)} collective-permute-done((f32[32,2048]{1,0:T(8,128)S(1)}, f32[32,2048]{1,0:T(8,128)S(1)}, u32[]{:S(2)}, u32[]{:S(2)}) %collective-permute-start.12) | collective-permute-done | bytes 262176 | tf_op jit(solution)/shard_map/ppermute | solution.py:17
  120.7 8.6 %collective-permute-done.13 = f32[32,2048]{1,0:T(8,128)S(1)} collective-permute-done((f32[32,2048]{1,0:T(8,128)S(1)}, f32[32,2048]{1,0:T(8,128)S(1)}, u32[]{:S(2)}, u32[]{:S(2)}) %collective-permute-start.13) | collective-permute-done | bytes 262176 | tf_op jit(solution)/shard_map/ppermute | solution.py:17
  133.0 3.5 %fusion = f32[32,24,128]{2,0,1:T(8,128)S(1)} fusion(f32[24,128,128]{2,1,0:T(8,128)S(1)} %copy-done, f32[24,32,128]{2,1,0:T(8,128)} %gather_fusion.3, pred[24]{0:T(512)(128)(4,1)S(1)} %iota_compare_fusion.4), kind=kOutput, calls=%fused_computation.9 | convolution fusion | flops 151093248 | bytes 2359320 | tf_op jit(solution)/shard_map/ktb,tab->kta/dot_general | solution.py:40
  137.9 15.0 %all-gather.2.cloned.1.call-done = f32[128,2048]{1,0:T(8,128)} async-done(((f32[32,2048]{1,0:T(8,128)}), f32[128,2048]{1,0:T(8,128)}) %all-gather.2.cloned.1.call-update) | async-done | bytes 1048592 | tf_op jit(solution)/shard_map/all_gather | solution.py:62
  155.4 37.1 %psum.7 = f32[32,128]{1,0:T(8,128)S(1)} all-reduce(f32[32,128]{1,0:T(8,128)S(1)} %fusion.31), channel_id=1, replica_groups=mesh['blk'=8,'col'=4] {'blk'}, use_global_device_ids=true, to_apply=%region_0.1 | all-reduce | flops 4096 | bytes 32768 | tf_op jit(solution)/shard_map/psum | solution.py:64
  192.6 5.2 %all_gather.7 = f32[128,128]{1,0:T(8,128)S(1)} all-gather(f32[32,128]{1,0:T(8,128)S(1)} %psum.7), channel_id=1, replica_groups=mesh['blk'=8,'col'=4] {'col'}, dimensions={0}, use_global_device_ids=true | all-gather | bytes 81920 | tf_op jit(solution)/shard_map/all_gather | solution.py:65
  197.9 11.7 %cholesky.17 = f32[128,128]{1,0:T(8,128)S(1)} custom-call(f32[128,128]{1,0:T(8,128)S(1)} %fusion.15), custom_call_target="Cholesky" | custom-call | tf_op jit(solution)/shard_map/jit(cholesky)/cholesky | solution.py:66
  211.6 9.8 %custom-call.6 = f32[1,128,128]{1,2,0:T(8,128)S(1)} custom-call(f32[1,128,128]{2,1,0:T(8,128)S(1)} %get-tuple-element.3), custom_call_target="InvertDiagBlocksLowerTriangular" | custom-call | tf_op jit(solution)/shard_map/triangular_solve | solution.py:69
  (77 shorter events, 40.1 us)
Async XLA Ops:
  7.2 30.9 %copy-start = (f32[24,128,128]{2,1,0:T(8,128)S(1)}, f32[24,128,128]{2,1,0:T(8,128)}, u32[]{:S(2)}) copy-start(f32[24,128,128]{2,1,0:T(8,128)} %param.6) | copy-start | bytes 4718596
  7.2 145.7 %all-gather.2.cloned.1.call-start = ((), (), s32[]{:S(2)}) async-start(), calls=%async_computation | async-start | bytes 1310720 | tf_op jit(solution)/shard_map/all_gather | solution.py:62
  7.2 14.5 %collective-permute-start = (f32[32,2048]{1,0:T(8,128)}, f32[32,2048]{1,0:T(8,128)S(1)}, u32[]{:S(2)}, u32[]{:S(2)}) collective-permute-start(f32[32,2048]{1,0:T(8,128)} %param.5), channel_id=1, source_target_pairs={{0,4},{4,8},{8,12},{12,16},{16,20},{20,24},{24,28},{28,0},{1,5},{5... | collective-permute-start | bytes 786440 | tf_op jit(solution)/shard_map/ppermute | solution.py:17
  10.2 14.5 %collective-permute-start.2 = (f32[32,2048]{1,0:T(8,128)}, f32[32,2048]{1,0:T(8,128)S(1)}, u32[]{:S(2)}, u32[]{:S(2)}) collective-permute-start(f32[32,2048]{1,0:T(8,128)} %param.5), channel_id=1, source_target_pairs={{0,28},{4,0},{8,4},{12,8},{16,12},{20,16},{24,20},{28,24},{1,29},{... | collective-permute-start | bytes 786440 | tf_op jit(solution)/shard_map/ppermute | solution.py:17
  21.7 12.7 %collective-permute-start.1 = (f32[32,2048]{1,0:T(8,128)S(1)}, f32[32,2048]{1,0:T(8,128)S(1)}, u32[]{:S(2)}, u32[]{:S(2)}) collective-permute-start(f32[32,2048]{1,0:T(8,128)S(1)} %collective-permute-done), channel_id=1, source_target_pairs={{0,4},{4,8},{8,12},{12,16},{16,20},{20,24},{24,28},{28,0},{1,5},{5... | collective-permute-start | bytes 786440 | tf_op jit(solution)/shard_map/ppermute | solution.py:17
  24.8 12.5 %collective-permute-start.3 = (f32[32,2048]{1,0:T(8,128)S(1)}, f32[32,2048]{1,0:T(8,128)S(1)}, u32[]{:S(2)}, u32[]{:S(2)}) collective-permute-start(f32[32,2048]{1,0:T(8,128)S(1)} %collective-permute-done.2), channel_id=1, source_target_pairs={{0,28},{4,0},{8,4},{12,8},{16,12},{20,16},{24,20},{28,24},{1,29},{... | collective-permute-start | bytes 786440 | tf_op jit(solution)/shard_map/ppermute | solution.py:17
  41.3 10.7 %collective-permute-start.4 = (f32[32,2048]{1,0:T(8,128)S(1)}, f32[32,2048]{1,0:T(8,128)S(1)}, u32[]{:S(2)}, u32[]{:S(2)}) collective-permute-start(f32[32,2048]{1,0:T(8,128)S(1)} %bitcast.99), channel_id=1, source_target_pairs={{0,4},{4,8},{8,12},{12,16},{16,20},{20,24},{24,28},{28,0},{1,5},{5... | collective-permute-start | bytes 786440 | tf_op jit(solution)/shard_map/ppermute | solution.py:17
  42.0 12.5 %collective-permute-start.6 = (f32[32,2048]{1,0:T(8,128)S(1)}, f32[32,2048]{1,0:T(8,128)S(1)}, u32[]{:S(2)}, u32[]{:S(2)}) collective-permute-start(f32[32,2048]{1,0:T(8,128)S(1)} %bitcast.100), channel_id=1, source_target_pairs={{0,28},{4,0},{8,4},{12,8},{16,12},{20,16},{24,20},{28,24},{1,29},{... | collective-permute-start | bytes 786440 | tf_op jit(solution)/shard_map/ppermute | solution.py:17
  52.0 10.7 %collective-permute-start.5 = (f32[32,2048]{1,0:T(8,128)S(1)}, f32[32,2048]{1,0:T(8,128)S(1)}, u32[]{:S(2)}, u32[]{:S(2)}) collective-permute-start(f32[32,2048]{1,0:T(8,128)S(1)} %collective-permute-done.4), channel_id=1, source_target_pairs={{0,4},{4,8},{8,12},{12,16},{16,20},{20,24},{24,28},{28,0},{1,5},{5... | collective-permute-start | bytes 786440 | tf_op jit(solution)/shard_map/ppermute | solution.py:17
  54.6 11.3 %collective-permute-start.7 = (f32[32,2048]{1,0:T(8,128)S(1)}, f32[32,2048]{1,0:T(8,128)S(1)}, u32[]{:S(2)}, u32[]{:S(2)}) collective-permute-start(f32[32,2048]{1,0:T(8,128)S(1)} %collective-permute-done.6), channel_id=1, source_target_pairs={{0,28},{4,0},{8,4},{12,8},{16,12},{20,16},{24,20},{28,24},{1,29},{... | collective-permute-start | bytes 786440 | tf_op jit(solution)/shard_map/ppermute | solution.py:17
  67.0 3.1 %copy-start.2 = (f32[32,2048]{1,0:T(8,128)S(1)}, f32[32,2048]{1,0:T(8,128)}, u32[]{:S(2)}) copy-start(f32[32,2048]{1,0:T(8,128)} %param.5) | copy-start | bytes 786436
  70.2 12.5 %collective-permute-start.8 = (f32[32,2048]{1,0:T(8,128)S(1)}, f32[32,2048]{1,0:T(8,128)S(1)}, u32[]{:S(2)}, u32[]{:S(2)}) collective-permute-start(f32[32,2048]{1,0:T(8,128)S(1)} %bitcast_subtract_fusion.2), channel_id=1, source_target_pairs={{0,4},{4,8},{8,12},{12,16},{16,20},{20,24},{24,28},{28,0},{1,5},{5... | collective-permute-start | bytes 786440 | tf_op jit(solution)/shard_map/ppermute | solution.py:17
  71.0 14.5 %collective-permute-start.10 = (f32[32,2048]{1,0:T(8,128)S(1)}, f32[32,2048]{1,0:T(8,128)S(1)}, u32[]{:S(2)}, u32[]{:S(2)}) collective-permute-start(f32[32,2048]{1,0:T(8,128)S(1)} %bitcast_subtract_fusion.2), channel_id=1, source_target_pairs={{0,28},{4,0},{8,4},{12,8},{16,12},{20,16},{24,20},{28,24},{1,29},{... | collective-permute-start | bytes 786440 | tf_op jit(solution)/shard_map/ppermute | solution.py:17
  82.8 10.2 %collective-permute-start.9 = (f32[32,2048]{1,0:T(8,128)S(1)}, f32[32,2048]{1,0:T(8,128)S(1)}, u32[]{:S(2)}, u32[]{:S(2)}) collective-permute-start(f32[32,2048]{1,0:T(8,128)S(1)} %collective-permute-done.8), channel_id=1, source_target_pairs={{0,4},{4,8},{8,12},{12,16},{16,20},{20,24},{24,28},{28,0},{1,5},{5... | collective-permute-start | bytes 786440 | tf_op jit(solution)/shard_map/ppermute | solution.py:17
  85.5 13.0 %collective-permute-start.11 = (f32[32,2048]{1,0:T(8,128)S(1)}, f32[32,2048]{1,0:T(8,128)S(1)}, u32[]{:S(2)}, u32[]{:S(2)}) collective-permute-start(f32[32,2048]{1,0:T(8,128)S(1)} %collective-permute-done.10), channel_id=1, source_target_pairs={{0,28},{4,0},{8,4},{12,8},{16,12},{20,16},{24,20},{28,24},{1,29},{... | collective-permute-start | bytes 786440 | tf_op jit(solution)/shard_map/ppermute | solution.py:17
  104.2 11.7 %collective-permute-start.12 = (f32[32,2048]{1,0:T(8,128)S(1)}, f32[32,2048]{1,0:T(8,128)S(1)}, u32[]{:S(2)}, u32[]{:S(2)}) collective-permute-start(f32[32,2048]{1,0:T(8,128)S(1)} %bitcast_subtract_fusion.1), channel_id=1, source_target_pairs={{0,4},{4,8},{8,12},{12,16},{16,20},{20,24},{24,28},{28,0},{1,5},{5... | collective-permute-start | bytes 786440 | tf_op jit(solution)/shard_map/ppermute | solution.py:17
  104.3 14.2 %collective-permute-start.14 = (f32[32,2048]{1,0:T(8,128)S(1)}, f32[32,2048]{1,0:T(8,128)S(1)}, u32[]{:S(2)}, u32[]{:S(2)}) collective-permute-start(f32[32,2048]{1,0:T(8,128)S(1)} %bitcast_subtract_fusion.1), channel_id=1, source_target_pairs={{0,28},{4,0},{8,4},{12,8},{16,12},{20,16},{24,20},{28,24},{1,29},{... | collective-permute-start | bytes 786440 | tf_op jit(solution)/shard_map/ppermute | solution.py:17
  115.9 13.3 %collective-permute-start.13 = (f32[32,2048]{1,0:T(8,128)S(1)}, f32[32,2048]{1,0:T(8,128)S(1)}, u32[]{:S(2)}, u32[]{:S(2)}) collective-permute-start(f32[32,2048]{1,0:T(8,128)S(1)} %collective-permute-done.12), channel_id=1, source_target_pairs={{0,4},{4,8},{8,12},{12,16},{16,20},{20,24},{24,28},{28,0},{1,5},{5... | collective-permute-start | bytes 786440 | tf_op jit(solution)/shard_map/ppermute | solution.py:17
  118.5 13.0 %collective-permute-start.15 = (f32[32,2048]{1,0:T(8,128)S(1)}, f32[32,2048]{1,0:T(8,128)S(1)}, u32[]{:S(2)}, u32[]{:S(2)}) collective-permute-start(f32[32,2048]{1,0:T(8,128)S(1)} %collective-permute-done.14), channel_id=1, source_target_pairs={{0,28},{4,0},{8,4},{12,8},{16,12},{20,16},{24,20},{28,24},{1,29},{... | collective-permute-start | bytes 786440 | tf_op jit(solution)/shard_map/ppermute | solution.py:17
  152.9 68.7 %copy-start.1 = (f32[128,2048]{1,0:T(8,128)S(1)}, f32[128,2048]{1,0:T(8,128)}, u32[]{:S(2)}) copy-start(f32[128,2048]{1,0:T(8,128)} %all-gather.2.cloned.1.call-done) | copy-start | bytes 3145732
Sparse Core Ops, SparseCore 0:
  138.0 14.8 all-gather.1
where the time goes:
time: 230 us
  waiting for transfers between devices  74.2 us (32%)
  starting transfers between devices  47.6 us (21%)
  blocking collectives  42.3 us (18%)
  other arithmetic  25.9 us (11%)
  matrix products  18.3 us (8%)
  between operations  15 us (7%)
  local copies, waits for them, and re-layouts  6.46 us (3%)
    ppermute x16, waiting for transfers between devices, shifted(): return lax.ppermute(value, axis, pairs)  59.2 us
    ppermute x16, starting transfers between devices, shifted(): return lax.ppermute(value, axis, pairs)  47.5 us
    psum x1, blocking collectives, per_device(): own_rows = lax.psum(partial_rows, 'blk')  37.1 us
    all_gather x1, waiting for transfers between devices, per_device(): all_columns = lax.all_gather(current, 'col', axis=0, tiled=True)  15 us
    another operation x3, other arithmetic, per_device(): factor = jnp.linalg.cholesky(gram)  12.4 us
    dot_general x4, matrix products, apply_graph(): jnp.einsum('ktb,tab->kta', piece, tile_values, precision=lax.Precision.HI...  12.1 us
    another operation x1, other arithmetic, per_device(): lax.linalg.triangular_solve(factor, jnp.eye(K, dtype=jnp.float32), left_s...  9.81 us
    all_gather x1, blocking collectives, per_device(): gram = lax.all_gather(own_rows, 'col', axis=0, tiled=True)  5.23 us
  transfers between devices with their start and end apart: 17, of which 15 were waited for; matrix products, arithmetic and copies ran while one was open for 1% of the time, Pallas kernels for 0%

commit v1 on v0

v1 whole, which is shorter than its diff:
```python
import functools

import jax
import jax.numpy as jnp
from jax import lax
from jax.experimental import pallas as pl
from jax.experimental.pallas import tpu as pltpu
from jax.sharding import PartitionSpec as P

REACH = 2
DEGREE = 4
HALVES = 2
UNROLL = 8
MESH = pl.DeviceIdType.MESH
NT = (((1,), (1,)), ((), ()))


def split(value):
    high = value.astype(jnp.bfloat16)
    low = (value - high.astype(jnp.float32)).astype(jnp.bfloat16)
    return jnp.concatenate([high, low], axis=0)


def folded(value):
    rows, columns = value.shape[0] // 2, value.shape[1] // 2
    return (value[:rows, :columns] + value[rows:, :columns]) + (
        value[:rows, columns:] + value[rows:, columns:]
    )


def filter_kernel(
    n, q, panel_ref, tiles_ref, cols_ref, weights_ref, full_ref, gram_ref,
    weights, contrib, full, part, pair, mine, sums, rows_all,
    halo_send, halo_recv, col_send, col_recv, pair_send, pair_recv,
    sum_send, sum_recv, row_send, row_recv, *windows,
):
    win = [windows[s * HALVES:(s + 1) * HALVES] for s in range(DEGREE)]

    p, c = lax.axis_index("blk"), lax.axis_index("col")
    tiles, bs = tiles_ref.shape[0], tiles_ref.shape[1]
    width = panel_ref.shape[0]
    rb = panel_ref.shape[1] // bs
    hw = width // HALVES
    odd = lax.rem(p, 2)
    mate = p + 1 - 2 * odd
    own = REACH * rb

    def blk(value):
        return {"blk": value}

    def away(steps):
        return lax.rem(p + steps + n, n)

    core = c + 1 - 2 * lax.rem(c, 2)
    cross = lax.rem(c + 2, q)

    barrier = pltpu.get_barrier_semaphore()
    for j in range(1, n // 2):
        pl.semaphore_signal(barrier, inc=1, device_id=blk(away(2 * j)), device_id_type=MESH)
    pl.semaphore_signal(barrier, inc=1, device_id=blk(mate), device_id_type=MESH)
    for j in range(1, q):
        pl.semaphore_signal(
            barrier, inc=1, device_id={"col": lax.rem(c + j, q)}, device_id_type=MESH
        )

    for h in range(HALVES):
        for r in range(rb):
            win[0][h][own + r] = panel_ref[h * hw:(h + 1) * hw, r * bs:(r + 1) * bs]
    pl.semaphore_wait(barrier, n // 2 - 1 + 1 + q - 1)

    def slot(s, h, index):
        return win[s][h].at[pl.ds(index * rb, rb)]

    def halo(s, h, j, src, dst, target):
        return pltpu.make_async_remote_copy(
            src_ref=slot(s, h, src), dst_ref=slot(s, h, dst),
            send_sem=halo_send.at[s, h, j], recv_sem=halo_recv.at[s, h, j],
            device_id=blk(target), device_id_type=MESH,
        )

    def send(s, h):
        halo(s, h, 0, REACH, 0, away(2)).start()
        halo(s, h, 1, REACH, 4, away(-2)).start()
        halo(s, h, 2, REACH, 1 + 2 * odd, mate).start()

    def forward(s, h):
        halo(s, h, 1 - odd, REACH, 4 - 4 * odd, mate).wait_recv()
        halo(s, h, 3, 4 - 4 * odd, 3 - 2 * odd, mate).start()

    def arrived(s, h):
        halo(s, h, odd, REACH, 4 * odd, mate).wait_recv()
        halo(s, h, 2, REACH, 3 - 2 * odd, mate).wait_recv()
        halo(s, h, 3, REACH, 1 + 2 * odd, mate).wait_recv()

    def apply(s, h):
        @pl.loop(0, tiles // UNROLL)
        def _(outer):
            for u in range(UNROLL):
                t = outer * UNROLL + u
                piece = split(win[s][h][cols_ref[t]])
                contrib[t] = folded(lax.dot_general(
                    piece, weights[t], NT, preferred_element_type=jnp.float32
                ))

        @pl.loop(0, rb)
        def _(r):
            total = weights_ref[r] * contrib[0]
            for t in range(1, tiles):
                total = total + weights_ref[t * rb + r] * contrib[t]
            if s > 0:
                total = 2.0 * total - win[s - 1][h][own + r]
            if s < DEGREE - 1:
                win[s + 1][h][own + r] = total
            else:
                full[r, pl.ds(pl.multiple_of(c * width + h * hw, hw), hw), :] = total

    for h in range(HALVES):
        send(0, h)

    @pl.loop(0, tiles)
    def _(t):
        weights[t] = split(tiles_ref[t])

    def rows_of(which, h):
        return full.at[:, pl.ds(pl.multiple_of(which * width + h * hw, hw), hw), :]

    def column(h, j, which, target):
        return pltpu.make_async_remote_copy(
            src_ref=rows_of(which, h), dst_ref=rows_of(which, h),
            send_sem=col_send.at[h, j], recv_sem=col_recv.at[h, j],
            device_id={"col": target}, device_id_type=MESH,
        )

    for s in range(DEGREE):
        for h in range(HALVES):
            forward(s, h)
            arrived(s, h)
            apply(s, h)
            if s < DEGREE - 1:
                send(s + 1, h)
            else:
                column(h, 0, c, cross).start()
                column(h, 1, c, core).start()

    crossed = lax.rem(core + 2, q)
    for h in range(HALVES):
        column(h, 0, cross, cross).wait_recv()
        column(h, 2, cross, core).start()
    for h in range(HALVES):
        column(h, 1, core, core).wait_recv()
        column(h, 2, crossed, core).wait_recv()

    part[...] = jnp.zeros_like(part)

    @pl.loop(0, rb)
    def _(r):
        rows = full[r, pl.ds(pl.multiple_of(c * width, width), width), :]
        part[...] += lax.dot_general(
            split(rows), split(full[r]), NT, preferred_element_type=jnp.float32
        )

    mine[...] = folded(part[...])
    exchange = pltpu.make_async_remote_copy(
        src_ref=mine, dst_ref=pair, send_sem=pair_send, recv_sem=pair_recv,
        device_id=blk(mate), device_id_type=MESH,
    )
    exchange.start()
    exchange.wait()

    z = lax.div(p, 2)
    sums[z] = mine[...] + pair[...]

    def total_copy(j, index, target):
        return pltpu.make_async_remote_copy(
            src_ref=sums.at[index], dst_ref=sums.at[index],
            send_sem=sum_send.at[j - 1], recv_sem=sum_recv.at[j - 1],
            device_id=blk(target), device_id_type=MESH,
        )

    for j in range(1, n // 2):
        total_copy(j, z, away(2 * j)).start()
    for j in range(1, n // 2):
        total_copy(j, lax.rem(z - j + n // 2, n // 2), mate).wait_recv()
    gram = sums[0]
    for j in range(1, n // 2):
        gram = gram + sums[j]

    place = pl.ds(pl.multiple_of(c * width, width), width)
    rows_all[place, :] = gram

    def row_copy(j, which, target):
        where = rows_all.at[pl.ds(pl.multiple_of(which * width, width), width), :]
        return pltpu.make_async_remote_copy(
            src_ref=where, dst_ref=where,
            send_sem=row_send.at[j - 1], recv_sem=row_recv.at[j - 1],
            device_id={"col": target}, device_id_type=MESH,
        )

    for j in range(1, q):
        row_copy(j, c, lax.rem(c + j, q)).start()

    @pl.loop(0, rb)
    def _(r):
        full_ref[r] = full[r]

    for j in range(1, q):
        row_copy(j, lax.rem(c - j + q, q), core).wait_recv()
    gram_ref[...] = rows_all[...]

    for s in range(DEGREE):
        for h in range(HALVES):
            for j in range(4):
                halo(s, h, j, REACH, 0, mate).wait_send()
    for h in range(HALVES):
        for j in range(3):
            column(h, j, c, core).wait_send()
    for j in range(1, n // 2):
        total_copy(j, z, mate).wait_send()
    for j in range(1, q):
        row_copy(j, c, core).wait_send()


def filtered_and_gram(n, q, panel, tile_values, local_cols, row_weights):
    width, vertices = panel.shape
    tiles, bs, _ = tile_values.shape
    rb = vertices // bs
    hw = width // HALVES
    k = width * q
    dma = pltpu.SemaphoreType.DMA
    vmem = pl.BlockSpec(memory_space=pltpu.VMEM)
    smem = pl.BlockSpec(memory_space=pltpu.SMEM)
    return pl.pallas_call(
        functools.partial(filter_kernel, n, q),
        out_shape=(
            jax.ShapeDtypeStruct((rb, k, bs), jnp.float32),
            jax.ShapeDtypeStruct((k, k), jnp.float32),
        ),
        in_specs=[vmem, vmem, smem, smem],
        out_specs=(vmem, vmem),
        scratch_shapes=[
            pltpu.VMEM((tiles, 2 * bs, bs), jnp.bfloat16),
            pltpu.VMEM((tiles, hw, bs), jnp.float32),
            pltpu.VMEM((rb, k, bs), jnp.float32),
            pltpu.VMEM((2 * width, 2 * k), jnp.float32),
            pltpu.VMEM((width, k), jnp.float32),
            pltpu.VMEM((width, k), jnp.float32),
            pltpu.VMEM((n // 2, width, k), jnp.float32),
            pltpu.VMEM((k, k), jnp.float32),
            dma((DEGREE, HALVES, 4)), dma((DEGREE, HALVES, 4)),
            dma((HALVES, 3)), dma((HALVES, 3)),
            dma, dma,
            dma((n // 2 - 1,)), dma((n // 2 - 1,)),
            dma((q - 1,)), dma((q - 1,)),
        ] + [pltpu.VMEM(((2 * REACH + 1) * rb, hw, bs), jnp.float32)] * (DEGREE * HALVES),
        compiler_params=pltpu.CompilerParams(
            collective_id=0, has_side_effects=True, vmem_limit_bytes=40 << 20
        ),
    )(panel, tile_values, local_cols, row_weights)


def per_device(start_panel, tile_values, tile_rows, tile_cols, tile_counts):
    position = lax.axis_index("blk")
    n, q = lax.axis_size("blk"), lax.axis_size("col")
    width, vertices = start_panel.shape
    tiles, bs, _ = tile_values.shape
    rb = vertices // bs
    local_cols = (tile_cols // rb - position + REACH + n) % n * rb + tile_cols % rb
    local_rows = tile_rows - position * rb
    live = jnp.arange(tiles, dtype=jnp.int32) < tile_counts[0]
    row_weights = (
        (local_rows[:, None] == jnp.arange(rb, dtype=jnp.int32)[None, :]) & live[:, None]
    ).astype(jnp.float32).reshape(-1)
    full, gram = filtered_and_gram(n, q, start_panel, tile_values, local_cols, row_weights)
    factor = jnp.linalg.cholesky(gram)
    scale = jnp.sqrt(jnp.asarray(vertices * n, jnp.float32))
    inverse = lax.linalg.triangular_solve(
        factor, jnp.eye(width * q, dtype=jnp.float32), left_side=True, lower=True
    )
    inverse_rows = lax.dynamic_slice_in_dim(inverse, lax.axis_index("col") * width, width, 0)
    ortho_panel = jnp.einsum(
        "ij,bjv->ibv", inverse_rows, full, precision=lax.Precision.HIGHEST
    ).reshape(width, vertices) * scale
    return (ortho_panel, factor / scale)


def solution(mesh):
    in_specs = (P("col", "blk"), P("blk", None, None), P("blk"), P("blk"), P("blk"))
    out_specs = (P("col", "blk"), P())
    return jax.shard_map(
        per_device, mesh=mesh, in_specs=in_specs, out_specs=out_specs, check_vma=False
    )
```

time: 230 us -> 122 us (0.53)
  Pallas kernels: 0 us -> 91.6 us
  waiting for transfers between devices: 74.2 us -> 0 us
  starting transfers between devices: 47.6 us -> 0 us
  blocking collectives: 42.3 us -> 0 us
  matrix products: 18.3 us -> 0.91 us
  between operations: 15 us -> 1.33 us
  local copies, waits for them, and re-layouts: 6.46 us -> 3.25 us
    pallas_call x0 -> x1, Pallas kernels: none -> 91.6 us  [filtered_and_gram(): pl.pallas_call(functools.partial(filter_kernel, n, q), out_shape=(jax.Sha...]
    ppermute x16 -> x0, waiting for transfers between devices: 59.2 us -> none  [shifted(): return lax.ppermute(value, axis, pairs)]
    ppermute x16 -> x0, starting transfers between devices: 47.5 us -> none  [shifted(): return lax.ppermute(value, axis, pairs)]
    psum x1 -> x0, blocking collectives: 37.1 us -> none  [per_device(): own_rows = lax.psum(partial_rows, 'blk')]
    dot_general x10 -> x1, matrix products: 18.1 us -> 0.66 us  [per_device(): jnp.einsum('ij,bjv->ibv', inverse_rows, full, precision=lax.Precision.HIG...]
    all_gather x1 -> x0, waiting for transfers between devices: 15 us -> none  [per_device(): all_columns = lax.all_gather(current, 'col', axis=0, tiled=True)]
    all_gather x1 -> x0, blocking collectives: 5.23 us -> none  [per_device(): gram = lax.all_gather(own_rows, 'col', axis=0, tiled=True)]
    gather x4 -> x0, local copies, waits for them, and re-layouts: 3.81 us -> none  [apply_graph(): piece = blocks[:, local_cols, :]]
  transfers between devices with their start and end apart: 17 -> 0, of which waited for: 15 -> 0; matrix products, arithmetic and copies ran while one was open for 1% -> 0% of each run, Pallas kernels for 0% -> 0%
where the time goes in v1:
time: 122 us
  Pallas kernels  91.6 us (75%)
  other arithmetic  24.9 us (20%)
  local copies, waits for them, and re-layouts  3.25 us (3%)
  between operations  1.33 us (1%)
    pallas_call x1, Pallas kernels, filtered_and_gram(): pl.pallas_call(functools.partial(filter_kernel, n, q), out_shape=(jax.Sha...  91.6 us
    another operation x3, other arithmetic, per_device(): factor = jnp.linalg.cholesky(gram)  12.4 us
    another operation x1, other arithmetic, per_device(): lax.linalg.triangular_solve(factor, jnp.eye(width * q, dtype=jnp.float32)...  9.81 us

profile of v1, /device:TPU:0, one launch (start us, length us, event | category | flops | bytes accessed | tf_op | source)
XLA Modules:
  0.0 122.0 jit_solution(4626749167860254161)
XLA Ops:
  1.3 0.7 fusion.9.cols_ref
  2.0 0.7 broadcast_subtract_fusion
  2.6 0.1 fusion.8
  2.7 0.1 reshape.29.weights_ref
  2.8 0.0 copy-start
  2.8 1.4 %copy-done = f32[24,128,128]{2,1,0:T(8,128)S(1)} copy-done((f32[24,128,128]{2,1,0:T(8,128)S(1)}, f32[24,128,128]{2,1,0:T(8,128)}, u32[]{:S(2)}) %copy-start) | copy-done | bytes 1572888
  4.2 0.0 copy-start.1
  4.2 0.9 copy-done.1
  5.2 91.6 %shard_map.68 = (f32[16,128,128]{2,1,0:T(8,128)S(1)}, f32[128,128]{1,0:T(8,128)S(1)}) custom-call(f32[32,2048]{1,0:T(8,128)S(1)} %copy-done.1, f32[24,128,128]{2,1,0:T(8,128)S(1)} %copy-done, s32[24]{0:T(128)S(1)} %fusion.9.cols_ref, f32[384]{0:T(512)S(1)} %reshape.29.weights_ref), custom_call_target="tpu_custom_call" | custom-call | tf_op jit(solution)/shard_map/pallas_call | solution.py:232
  96.8 0.1 copy.8
  96.9 11.7 %cholesky.17 = f32[128,128]{1,0:T(8,128)S(1)} custom-call(f32[128,128]{1,0:T(8,128)S(1)} %fusion.3), custom_call_target="Cholesky" | custom-call | tf_op jit(solution)/shard_map/jit(cholesky)/cholesky | solution.py:274
  108.6 0.6 compare_reduce_fusion
  109.3 1.3 %fusion.4 = (f32[128,128]{1,0:T(8,128)}, f32[1,128,128]{2,1,0:T(8,128)S(1)}) fusion(f32[128,128]{1,0:T(8,128)S(1)} %cholesky.17, pred[]{:T(512)} %compare_reduce_fusion), kind=kLoop, calls=%fused_computation.12 | loop fusion | flops 81920 | bytes 196609 | tf_op jit(solution)/shard_map/div | solution.py:283
  110.6 9.8 %custom-call.6 = f32[1,128,128]{1,2,0:T(8,128)S(1)} custom-call(f32[1,128,128]{2,1,0:T(8,128)S(1)} %get-tuple-element.7), custom_call_target="InvertDiagBlocksLowerTriangular" | custom-call | tf_op jit(solution)/shard_map/triangular_solve | solution.py:276
  120.4 0.2 fusion.1
  120.6 0.7 fusion
  121.3 0.7 copy.12
  (3 shorter events, 0.1 us)
Async XLA Ops:
  2.8 1.4 %copy-start = (f32[24,128,128]{2,1,0:T(8,128)S(1)}, f32[24,128,128]{2,1,0:T(8,128)}, u32[]{:S(2)}) copy-start(f32[24,128,128]{2,1,0:T(8,128)} %tiles_ref.1) | copy-start | bytes 4718596
  4.2 0.9 copy-start.1

commit v2 on v1

--- a/solution.py
+++ b/solution.py
@@ -1,4 +1,5 @@
 import functools
+import math
 
 import jax
 import jax.numpy as jnp
@@ -10,6 +11,7 @@
 REACH = 2
 DEGREE = 4
 HALVES = 2
+PIECES = 4
 UNROLL = 8
 MESH = pl.DeviceIdType.MESH
 NT = (((1,), (1,)), ((), ()))
@@ -44,6 +46,7 @@
     odd = lax.rem(p, 2)
     mate = p + 1 - 2 * odd
     own = REACH * rb
+    span = rb // PIECES
 
     def blk(value):
         return {"blk": value}
@@ -68,29 +71,33 @@
             win[0][h][own + r] = panel_ref[h * hw:(h + 1) * hw, r * bs:(r + 1) * bs]
     pl.semaphore_wait(barrier, n // 2 - 1 + 1 + q - 1)
 
-    def slot(s, h, index):
-        return win[s][h].at[pl.ds(index * rb, rb)]
-
-    def halo(s, h, j, src, dst, target):
+    def slot(s, h, index, piece):
+        return win[s][h].at[pl.ds(index * rb + piece * span, span)]
+
+    def halo(s, h, j, piece, src, dst, target):
         return pltpu.make_async_remote_copy(
-            src_ref=slot(s, h, src), dst_ref=slot(s, h, dst),
-            send_sem=halo_send.at[s, h, j], recv_sem=halo_recv.at[s, h, j],
+            src_ref=slot(s, h, src, piece), dst_ref=slot(s, h, dst, piece),
+            send_sem=halo_send.at[s, h, j, piece], recv_sem=halo_recv.at[s, h, j, piece],
             device_id=blk(target), device_id_type=MESH,
         )
 
     def send(s, h):
-        halo(s, h, 0, REACH, 0, away(2)).start()
-        halo(s, h, 1, REACH, 4, away(-2)).start()
-        halo(s, h, 2, REACH, 1 + 2 * odd, mate).start()
+        for piece in range(PIECES):
+            halo(s, h, 1 - odd, piece, REACH, 4 - 4 * odd, away(4 * odd - 2)).start()
+            halo(s, h, odd, piece, REACH, 4 * odd, away(2 - 4 * odd)).start()
+        for piece in range(PIECES):
+            halo(s, h, 2, piece, REACH, 1 + 2 * odd, mate).start()
 
     def forward(s, h):
-        halo(s, h, 1 - odd, REACH, 4 - 4 * odd, mate).wait_recv()
-        halo(s, h, 3, 4 - 4 * odd, 3 - 2 * odd, mate).start()
+        for piece in range(PIECES):
+            halo(s, h, 1 - odd, piece, REACH, 4 - 4 * odd, mate).wait_recv()
+            halo(s, h, 3, piece, 4 - 4 * odd, 3 - 2 * odd, mate).start()
 
     def arrived(s, h):
-        halo(s, h, odd, REACH, 4 * odd, mate).wait_recv()
-        halo(s, h, 2, REACH, 3 - 2 * odd, mate).wait_recv()
-        halo(s, h, 3, REACH, 1 + 2 * odd, mate).wait_recv()
+        for piece in range(PIECES):
+            halo(s, h, odd, piece, REACH, 4 * odd, mate).wait_recv()
+            halo(s, h, 2, piece, REACH, 3 - 2 * odd, mate).wait_recv()
+            halo(s, h, 3, piece, REACH, 1 + 2 * odd, mate).wait_recv()
 
     def apply(s, h):
         @pl.loop(0, tiles // UNROLL)
@@ -210,7 +217,8 @@
     for s in range(DEGREE):
         for h in range(HALVES):
             for j in range(4):
-                halo(s, h, j, REACH, 0, mate).wait_send()
+                for piece in range(PIECES):
+                    halo(s, h, j, piece, REACH, 0, mate).wait_send()
     for h in range(HALVES):
         for j in range(3):
             column(h, j, c, core).wait_send()
@@ -246,7 +254,7 @@
             pltpu.VMEM((width, k), jnp.float32),
             pltpu.VMEM((n // 2, width, k), jnp.float32),
             pltpu.VMEM((k, k), jnp.float32),
-            dma((DEGREE, HALVES, 4)), dma((DEGREE, HALVES, 4)),
+            dma((DEGREE, HALVES, 4, PIECES)), dma((DEGREE, HALVES, 4, PIECES)),
             dma((HALVES, 3)), dma((HALVES, 3)),
             dma, dma,
             dma((n // 2 - 1,)), dma((n // 2 - 1,)),
@@ -256,6 +264,88 @@
             collective_id=0, has_side_effects=True, vmem_limit_bytes=40 << 20
         ),
     )(panel, tile_values, local_cols, row_weights)
+
+
+def split_three(value):
+    first = value.astype(jnp.bfloat16)
+    rest = value - first.astype(jnp.float32)
+    second = rest.astype(jnp.bfloat16)
+    third = (rest - second.astype(jnp.float32)).astype(jnp.bfloat16)
+    return first, second, third
+
+
+def factor_kernel(root, gram_ref, full_ref, ortho_ref, factor_ref, work, upper, inverse):
+    k = gram_ref.shape[0]
+    rb, bs = full_ref.shape[0], full_ref.shape[2]
+    width = ortho_ref.shape[0]
+    group = 8
+    row_index = lax.broadcasted_iota(jnp.int32, (k, k), 0)
+    lane_index = lax.broadcasted_iota(jnp.int32, (k, k), 1)
+    work[:, :k] = gram_ref[...]
+    work[:, k:] = jnp.where(row_index == lane_index, 1.0, 0.0)
+    sub = lax.broadcasted_iota(jnp.int32, (group, k), 0)
+    lane = lax.broadcasted_iota(jnp.int32, (group, k), 1)
+    for start in range(0, k, group):
+        left = work[start:start + group, :k]
+        right = work[start:start + group, k:]
+        columns = [
+            jnp.broadcast_to(left[:, start + j:start + j + 1], (group, k)) for j in range(group)
+        ]
+        pivots = jnp.ones((group, k), jnp.float32)
+        for j in range(group):
+            pivot = jnp.broadcast_to(columns[j][j:j + 1, :], (group, k))
+            pivots = jnp.where(sub == j, pivot, pivots)
+            if j < group - 1:
+                factor = jnp.where(sub > j, columns[j] / pivot, 0.0)
+                for m in range(j + 1, group):
+                    columns[m] = columns[m] - factor * columns[m][j:j + 1, :]
+                left = left - factor * left[j:j + 1, :]
+                right = right - factor * right[j:j + 1, :]
+        scale = lax.rsqrt(pivots)
+        scale = scale * (1.5 - (0.5 * pivots * scale) * scale)
+        left = jnp.where(lane >= sub + start, left * scale, 0.0)
+        right = right * scale
+        upper[start:start + group, :] = left
+        inverse[start:start + group, :] = right
+        if start + group < k:
+            a, b, c = split_three(left)
+            x, y, z = split_three(jnp.concatenate([left, right], axis=1))
+            work[...] -= lax.dot_general(
+                jnp.concatenate([a, a, b, a, b, c], axis=0),
+                jnp.concatenate([x, y, x, z, y, x], axis=0),
+                (((0,), (0,)), ((), ())), preferred_element_type=jnp.float32,
+            )
+    factor_ref[...] = upper[...].T * (1.0 / root)
+    place = pl.ds(pl.multiple_of(lax.axis_index("col") * width, width), width)
+    rows = split(inverse[place, :] * root)
+    for r in range(rb):
+        block = full_ref[r]
+        high = block.astype(jnp.bfloat16)
+        low = (block - high.astype(jnp.float32)).astype(jnp.bfloat16)
+        ortho_ref[:, r * bs:(r + 1) * bs] = folded(jnp.dot(
+            rows, jnp.concatenate([high, low], axis=1), preferred_element_type=jnp.float32
+        ))
+
+
+def factor_and_ortho(root, width, gram, full):
+    k = gram.shape[0]
+    rb, _, bs = full.shape
+    vmem = pl.BlockSpec(memory_space=pltpu.VMEM)
+    return pl.pallas_call(
+        functools.partial(factor_kernel, root),
+        out_shape=(
+            jax.ShapeDtypeStruct((width, rb * bs), jnp.float32),
+            jax.ShapeDtypeStruct((k, k), jnp.float32),
+        ),
+        in_specs=[vmem, vmem],
+        out_specs=(vmem, vmem),
+        scratch_shapes=[
+            pltpu.VMEM((k, 2 * k), jnp.float32),
+            pltpu.VMEM((k, k), jnp.float32),
+            pltpu.VMEM((k, k), jnp.float32),
+        ],
+        compiler_params=pltpu.CompilerParams(vmem_limit_bytes=24 << 20),
+    )(gram, full)
 
 
 def per_device(start_panel, tile_values, tile_rows, tile_cols, tile_counts):
@@ -271,16 +361,7 @@
         (local_rows[:, None] == jnp.arange(rb, dtype=jnp.int32)[None, :]) & live[:, None]
     ).astype(jnp.float32).reshape(-1)
     full, gram = filtered_and_gram(n, q, start_panel, tile_values, local_cols, row_weights)
-    factor = jnp.linalg.cholesky(gram)
-    scale = jnp.sqrt(jnp.asarray(vertices * n, jnp.float32))
-    inverse = lax.linalg.triangular_solve(
-        factor, jnp.eye(width * q, dtype=jnp.float32), left_side=True, lower=True
-    )
-    inverse_rows = lax.dynamic_slice_in_dim(inverse, lax.axis_index("col") * width, width, 0)
-    ortho_panel = jnp.einsum(
-        "ij,bjv->ibv", inverse_rows, full, precision=lax.Precision.HIGHEST
-    ).reshape(width, vertices) * scale
-    return (ortho_panel, factor / scale)
+    return factor_and_ortho(math.sqrt(vertices * n), width, gram, full)
 
 
 def solution(mesh):

time: 122 us -> 103 us (0.84)
  other arithmetic: 24.9 us -> 1.42 us
  Pallas kernels: 91.6 us -> 98 us
    another operation x4 -> x0, other arithmetic: 22.2 us -> none  [the longest x3 12.4 us: per_device(): factor = jnp.linalg.cholesky(gram)]
    pallas_call x0 -> x1, Pallas kernels: none -> 6.87 us  [factor_and_ortho(): pl.pallas_call(functools.partial(factor_kernel, root), out_shape=(jax.Sha...]
    div x2 -> x0, other arithmetic: 1.3 us -> none  [the longest x1 1.29 us: per_device(): return (ortho_panel, factor / scale)]
where the time goes in v2:
time: 103 us
  Pallas kernels  98 us (95%)
  local copies, waits for them, and re-layouts  2.44 us (2%)
  other arithmetic  1.42 us (1%)
  between operations  1.3 us (1%)
    pallas_call x1, Pallas kernels, filtered_and_gram(): pl.pallas_call(functools.partial(filter_kernel, n, q), out_shape=(jax.Sha...  91.1 us
    pallas_call x1, Pallas kernels, factor_and_ortho(): pl.pallas_call(functools.partial(factor_kernel, root), out_shape=(jax.Sha...  6.87 us
    unnamed x4, local copies, waits for them, and re-layouts  2.36 us

profile of v2, /device:TPU:0, one launch (start us, length us, event | category | flops | bytes accessed | tf_op | source)
XLA Modules:
  0.0 103.2 jit_solution(2470463361002602432)
XLA Ops:
  1.3 0.7 fusion.2.cols_ref
  2.0 0.7 broadcast_subtract_fusion
  2.6 0.1 fusion.1
  2.7 0.1 reshape.17.weights_ref
  2.8 0.0 copy-start
  2.8 1.4 %copy-done = f32[24,128,128]{2,1,0:T(8,128)S(1)} copy-done((f32[24,128,128]{2,1,0:T(8,128)S(1)}, f32[24,128,128]{2,1,0:T(8,128)}, u32[]{:S(2)}) %copy-start) | copy-done | bytes 1572888
  4.2 0.0 copy-start.1
  4.2 0.9 copy-done.1
  5.2 91.1 %shard_map.68 = (f32[16,128,128]{2,1,0:T(8,128)S(1)}, f32[128,128]{1,0:T(8,128)S(1)}) custom-call(f32[32,2048]{1,0:T(8,128)S(1)} %copy-done.1, f32[24,128,128]{2,1,0:T(8,128)S(1)} %copy-done, s32[24]{0:T(128)S(1)} %fusion.2.cols_ref, f32[384]{0:T(512)S(1)} %reshape.17.weights_ref), custom_call_target="tpu_custom_call" | custom-call | tf_op jit(solution)/shard_map/pallas_call | solution.py:240
  96.3 6.9 %shard_map.69 = (f32[32,2048]{1,0:T(8,128)}, f32[128,128]{1,0:T(8,128)}) custom-call(f32[128,128]{1,0:T(8,128)S(1)} %get-tuple-element.4.gram_ref, f32[16,128,128]{2,1,0:T(8,128)S(1)} %get-tuple-element.5.full_ref), custom_call_target="tpu_custom_call" | custom-call | tf_op jit(solution)/shard_map/pallas_call | solution.py:334
  (1 shorter events, 0.0 us)
Async XLA Ops:
  2.8 1.4 %copy-start = (f32[24,128,128]{2,1,0:T(8,128)S(1)}, f32[24,128,128]{2,1,0:T(8,128)}, u32[]{:S(2)}) copy-start(f32[24,128,128]{2,1,0:T(8,128)} %tiles_ref.1) | copy-start | bytes 4718596
  4.2 0.9 copy-start.1

commit v3 on v2

--- a/solution.py
+++ b/solution.py
@@ -85,6 +85,8 @@
         for piece in range(PIECES):
             halo(s, h, 1 - odd, piece, REACH, 4 - 4 * odd, away(4 * odd - 2)).start()
             halo(s, h, odd, piece, REACH, 4 * odd, away(2 - 4 * odd)).start()
+
+    def send_mate(s, h):
         for piece in range(PIECES):
             halo(s, h, 2, piece, REACH, 1 + 2 * odd, mate).start()
 
@@ -123,6 +125,7 @@
 
     for h in range(HALVES):
         send(0, h)
+        send_mate(0, h)
 
     @pl.loop(0, tiles)
     def _(t):
@@ -138,9 +141,9 @@
             device_id={"col": target}, device_id_type=MESH,
         )
 
+    forward(0, 0)
     for s in range(DEGREE):
         for h in range(HALVES):
-            forward(s, h)
             arrived(s, h)
             apply(s, h)
             if s < DEGREE - 1:
@@ -148,6 +151,12 @@
             else:
                 column(h, 0, c, cross).start()
                 column(h, 1, c, core).start()
+            if h < HALVES - 1:
+                forward(s, h + 1)
+            elif s < DEGREE - 1:
+                forward(s + 1, 0)
+            if s < DEGREE - 1:
+                send_mate(s + 1, h)
 
     crossed = lax.rem(core + 2, q)
     for h in range(HALVES):

time: 103 us -> 90.2 us (0.88)
  Pallas kernels: 98 us -> 84.8 us
    pallas_call x1, Pallas kernels: 91.1 us -> 78 us  [filtered_and_gram(): pl.pallas_call(functools.partial(filter_kernel, n, q), out_shape=(jax.Sha...]
where the time goes in v3:
time: 90.2 us; the launch traced here: 90 us
  Pallas kernels  84.8 us (94%)
  local copies, waits for them, and re-layouts  2.44 us (3%)
  other arithmetic  1.42 us (2%)
  between operations  1.3 us (1%)
    pallas_call x1, Pallas kernels, filtered_and_gram(): pl.pallas_call(functools.partial(filter_kernel, n, q), out_shape=(jax.Sha...  78 us
    pallas_call x1, Pallas kernels, factor_and_ortho(): pl.pallas_call(functools.partial(factor_kernel, root), out_shape=(jax.Sha...  6.86 us
    unnamed x4, local copies, waits for them, and re-layouts  2.36 us

profile of v3, /device:TPU:0, one launch (start us, length us, event | category | flops | bytes accessed | tf_op | source)
XLA Modules:
  0.0 90.0 jit_solution(4126631511765608513)
XLA Ops:
  1.3 0.7 fusion.2.cols_ref
  2.0 0.7 broadcast_subtract_fusion
  2.6 0.1 fusion.1
  2.7 0.1 reshape.17.weights_ref
  2.8 0.0 copy-start
  2.8 1.4 %copy-done = f32[24,128,128]{2,1,0:T(8,128)S(1)} copy-done((f32[24,128,128]{2,1,0:T(8,128)S(1)}, f32[24,128,128]{2,1,0:T(8,128)}, u32[]{:S(2)}) %copy-start) | copy-done | bytes 1572888
  4.2 0.0 copy-start.1
  4.2 0.9 %copy-done.1 = f32[32,2048]{1,0:T(8,128)S(1)} copy-done((f32[32,2048]{1,0:T(8,128)S(1)}, f32[32,2048]{1,0:T(8,128)}, u32[]{:S(2)}) %copy-start.1) | copy-done | bytes 262168
  5.2 78.0 %shard_map.68 = (f32[16,128,128]{2,1,0:T(8,128)S(1)}, f32[128,128]{1,0:T(8,128)S(1)}) custom-call(f32[32,2048]{1,0:T(8,128)S(1)} %copy-done.1, f32[24,128,128]{2,1,0:T(8,128)S(1)} %copy-done, s32[24]{0:T(128)S(1)} %fusion.2.cols_ref, f32[384]{0:T(512)S(1)} %reshape.17.weights_ref), custom_call_target="tpu_custom_call" | custom-call | tf_op jit(solution)/shard_map/pallas_call | solution.py:249
  83.1 6.9 %shard_map.69 = (f32[32,2048]{1,0:T(8,128)}, f32[128,128]{1,0:T(8,128)}) custom-call(f32[128,128]{1,0:T(8,128)S(1)} %get-tuple-element.4.gram_ref, f32[16,128,128]{2,1,0:T(8,128)S(1)} %get-tuple-element.5.full_ref), custom_call_target="tpu_custom_call" | custom-call | tf_op jit(solution)/shard_map/pallas_call | solution.py:343
  (1 shorter events, 0.0 us)
Async XLA Ops:
  2.8 1.4 %copy-start = (f32[24,128,128]{2,1,0:T(8,128)S(1)}, f32[24,128,128]{2,1,0:T(8,128)}, u32[]{:S(2)}) copy-start(f32[24,128,128]{2,1,0:T(8,128)} %tiles_ref.1) | copy-start | bytes 4718596
  4.2 0.9 %copy-start.1 = (f32[32,2048]{1,0:T(8,128)S(1)}, f32[32,2048]{1,0:T(8,128)}, u32[]{:S(2)}) copy-start(f32[32,2048]{1,0:T(8,128)} %panel_ref.1) | copy-start | bytes 786436

commit v4 on v3

--- a/solution.py
+++ b/solution.py
@@ -11,7 +11,7 @@
 REACH = 2
 DEGREE = 4
 HALVES = 2
-PIECES = 4
+PIECES = 2
 UNROLL = 8
 MESH = pl.DeviceIdType.MESH
 NT = (((1,), (1,)), ((), ()))
@@ -31,8 +31,8 @@
 
 
 def filter_kernel(
-    n, q, panel_ref, tiles_ref, cols_ref, weights_ref, full_ref, gram_ref,
-    weights, contrib, full, part, pair, mine, sums, rows_all,
+    n, q, panel_ref, tiles_hbm, cols_ref, weights_ref, full_ref, gram_ref,
+    tiles_ref, tiles_sem, weights, contrib, full, part, pair, mine, sums, rows_all,
     halo_send, halo_recv, col_send, col_recv, pair_send, pair_recv,
     sum_send, sum_recv, row_send, row_recv, *windows,
 ):
@@ -57,6 +57,8 @@
     core = c + 1 - 2 * lax.rem(c, 2)
     cross = lax.rem(c + 2, q)
 
+    fetch = pltpu.make_async_copy(tiles_hbm, tiles_ref, tiles_sem)
+    fetch.start()
     barrier = pltpu.get_barrier_semaphore()
     for j in range(1, n // 2):
         pl.semaphore_signal(barrier, inc=1, device_id=blk(away(2 * j)), device_id_type=MESH)
@@ -126,6 +128,8 @@
     for h in range(HALVES):
         send(0, h)
         send_mate(0, h)
+
+    fetch.wait()
 
     @pl.loop(0, tiles)
     def _(t):
@@ -252,9 +256,10 @@
             jax.ShapeDtypeStruct((rb, k, bs), jnp.float32),
             jax.ShapeDtypeStruct((k, k), jnp.float32),
         ),
-        in_specs=[vmem, vmem, smem, smem],
+        in_specs=[vmem, pl.BlockSpec(memory_space=pltpu.HBM), smem, smem],
         out_specs=(vmem, vmem),
         scratch_shapes=[
+            pltpu.VMEM((tiles, bs, bs), jnp.float32), dma,
             pltpu.VMEM((tiles, 2 * bs, bs), jnp.bfloat16),
             pltpu.VMEM((tiles, hw, bs), jnp.float32),
             pltpu.VMEM((rb, k, bs), jnp.float32),

time: 90.2 us -> 87.5 us (0.970)
  Pallas kernels: 84.8 us -> 82.1 us
    pallas_call x1, Pallas kernels: 78 us -> 75.2 us  [filtered_and_gram(): pl.pallas_call(functools.partial(filter_kernel, n, q), out_shape=(jax.Sha...]
where the time goes in v4:
time: 87.5 us; the launch traced here: 87.3 us
  Pallas kernels  82.1 us (94%)
  local copies, waits for them, and re-layouts  2.44 us (3%)
  other arithmetic  1.42 us (2%)
  between operations  1.3 us (1%)
    pallas_call x1, Pallas kernels, filtered_and_gram(): pl.pallas_call(functools.partial(filter_kernel, n, q), out_shape=(jax.Sha...  75.2 us
    pallas_call x1, Pallas kernels, factor_and_ortho(): pl.pallas_call(functools.partial(factor_kernel, root), out_shape=(jax.Sha...  6.86 us
    unnamed x4, local copies, waits for them, and re-layouts  2.36 us

profile of v4, /device:TPU:0, one launch (start us, length us, event | category | flops | bytes accessed | tf_op | source)
XLA Modules:
  0.0 87.3 jit_solution(18273146691356668772)
XLA Ops:
  1.3 0.7 fusion.2.cols_ref
  2.0 0.7 broadcast_subtract_fusion
  2.6 0.1 fusion.1
  2.7 0.1 reshape.17.weights_ref
  2.8 0.0 copy-start
  2.8 1.4 %copy-done = f32[24,128,128]{2,1,0:T(8,128)S(1)} copy-done((f32[24,128,128]{2,1,0:T(8,128)S(1)}, f32[24,128,128]{2,1,0:T(8,128)}, u32[]{:S(2)}) %copy-start) | copy-done | bytes 1572888
  4.2 0.0 copy-start.1
  4.2 0.9 %copy-done.1 = f32[32,2048]{1,0:T(8,128)S(1)} copy-done((f32[32,2048]{1,0:T(8,128)S(1)}, f32[32,2048]{1,0:T(8,128)}, u32[]{:S(2)}) %copy-start.1) | copy-done | bytes 262168
  5.2 75.2 %shard_map.68 = (f32[16,128,128]{2,1,0:T(8,128)S(1)}, f32[128,128]{1,0:T(8,128)S(1)}) custom-call(f32[32,2048]{1,0:T(8,128)S(1)} %copy-done.1, f32[24,128,128]{2,1,0:T(8,128)S(1)} %copy-done, s32[24]{0:T(128)S(1)} %fusion.2.cols_ref, f32[384]{0:T(512)S(1)} %reshape.17.weights_ref), custom_call_target="tpu_custom_call" | custom-call | tf_op jit(solution)/shard_map/pallas_call | solution.py:253
  80.4 6.9 %shard_map.69 = (f32[32,2048]{1,0:T(8,128)}, f32[128,128]{1,0:T(8,128)}) custom-call(f32[128,128]{1,0:T(8,128)S(1)} %get-tuple-element.4.gram_ref, f32[16,128,128]{2,1,0:T(8,128)S(1)} %get-tuple-element.5.full_ref), custom_call_target="tpu_custom_call" | custom-call | tf_op jit(solution)/shard_map/pallas_call | solution.py:348
  (1 shorter events, 0.0 us)
Async XLA Ops:
  2.8 1.4 %copy-start = (f32[24,128,128]{2,1,0:T(8,128)S(1)}, f32[24,128,128]{2,1,0:T(8,128)}, u32[]{:S(2)}) copy-start(f32[24,128,128]{2,1,0:T(8,128)} %tiles_hbm.1) | copy-start | bytes 4718596
  4.2 0.9 %copy-start.1 = (f32[32,2048]{1,0:T(8,128)S(1)}, f32[32,2048]{1,0:T(8,128)}, u32[]{:S(2)}) copy-start(f32[32,2048]{1,0:T(8,128)} %panel_ref.1) | copy-start | bytes 786436
